TPU v7x, 512 devices: a whole 4x8x8 slice. The times are simulated.
512 devices in a mesh: dp: 512 (over y, z, x, core).
Axes of the slice: x: 4, y: 8, z: 8, core: 2. Of those that a mesh axis runs over, the one named last changes fastest.
Arguments:
- features: bfloat16 [65536, 1024], P('dp')
- head_rows: bfloat16 [1024, 1024], P('dp')
- poses: bfloat16 [65536, 1024], P('dp')
- match_ids: int32 [65536], replicated, may hold values from 0 to 65535, as said below
- logit_scale: float32 [1], replicated, may hold values from 5 to 10
- logit_bias: float32 [1], replicated, may hold values from -4 to -2
Outputs:
- pose_grad: bfloat16 [65536, 1024], P('dp')
- head_grad: float32 [1024, 1024], P('dp')
- loss_terms: float32 [2], replicated
- scale_grad: float32 [1], replicated
Inputs may be any that keep to these rules, and one draw needn't show every extreme that they name: `match_ids`: samples with equal ids are positive pairs; every sample matches itself.
All inputs are finite; a program needn't handle non-finite values.
Results may differ from a plain program's by a relative error of at most 0.006.
Values may be sent and summed in bfloat16 or wider, within the bound.
A program may use at most 64 MiB of HBM per device.

v0:
```python
import jax
import jax.numpy as jnp
from jax import lax
from jax.sharding import PartitionSpec as P

REACH = 2


EPS = 1e-06


def passed_along(array, axis, by):
    length = lax.axis_size(axis)
    return lax.ppermute(array, axis, [(i, (i + by) % length) for i in range(length)])


def tile_terms(left_emb, left_ids, right_emb, right_ids, scale_val, bias_val):
    inner = lax.dot_general(
        left_emb, right_emb, (((1,), (1,)), ((), ())), preferred_element_type=jnp.float32
    )
    logits = scale_val * inner + bias_val
    matched = left_ids[:, None] == right_ids[None, :]
    sign_table = jnp.where(matched, jnp.float32(1.0), jnp.float32(-1.0))
    loss_sum = -jnp.sum(jax.nn.log_sigmoid(sign_table * logits))
    gradient = jax.nn.sigmoid(logits) - matched.astype(jnp.float32)
    weight = (scale_val * gradient).astype(jnp.bfloat16)
    totals = jnp.stack([loss_sum, jnp.sum(gradient), jnp.sum(gradient * inner)])
    return (weight, totals)


def pose_side(weight, left_emb):
    return lax.dot_general(
        weight, left_emb, (((0,), (0,)), ((), ())), preferred_element_type=jnp.float32
    )


def move_poses(pose_block, hop_by):
    return passed_along(pose_block, "dp", hop_by)


def move_grads(carried, hop_by):
    return passed_along(carried, "dp", hop_by)


def local(features, head_rows, poses, match_ids, logit_scale, logit_bias):
    row_count = features.shape[0]
    dev_count = lax.axis_size("dp")
    position = lax.axis_index("dp")
    head_full = lax.all_gather(head_rows, "dp", axis=0, tiled=True)
    proj = jnp.dot(features, head_full, preferred_element_type=jnp.float32)
    norm_img = jnp.sqrt(jnp.sum(proj * proj, axis=1, keepdims=True) + EPS)
    unit_img = proj / norm_img
    image_emb = unit_img.astype(jnp.bfloat16)
    pose_float = poses.astype(jnp.float32)
    norm_pose = jnp.sqrt(jnp.sum(pose_float * pose_float, axis=1, keepdims=True) + EPS)
    unit_pose = pose_float / norm_pose
    pose_emb = unit_pose.astype(jnp.bfloat16)
    scale_val = logit_scale[0]
    bias_val = logit_bias[0]

    def block_ids(offset):
        first = (position + offset) % dev_count * row_count
        return lax.dynamic_slice_in_dim(match_ids, first, row_count)

    own_ids = block_ids(0)
    streams = [(-REACH, REACH)] + [(1, REACH - number) for number in range(1, 2 * REACH + 1)]
    totals = jnp.zeros((3,), jnp.float32)
    grad_img = jnp.zeros(proj.shape, jnp.float32)
    pose_block = pose_emb
    carried = None
    last_offset = 0
    for hop_by, offset in streams:
        pose_block = move_poses(pose_block, hop_by)
        if carried is not None:
            carried = move_grads(carried, hop_by)
        weight, partial_value = tile_terms(
            image_emb, own_ids, pose_block, block_ids(offset), scale_val, bias_val
        )
        totals = totals + partial_value
        grad_img = grad_img + jnp.dot(weight, pose_block, preferred_element_type=jnp.float32)
        pose_term = pose_side(weight, image_emb)
        carried = pose_term if carried is None else carried + pose_term
        last_offset = offset
    grad_pose = move_grads(carried, last_offset)
    summed = lax.psum(totals, "dp")
    loss_terms = summed[:2] / match_ids.shape[0]
    scale_grad = summed[2:] / match_ids.shape[0]
    along_img = jnp.sum(unit_img * grad_img, axis=1, keepdims=True)
    grad_proj = ((grad_img - unit_img * along_img) / norm_img).astype(jnp.bfloat16)
    head_grad = lax.psum_scatter(
        lax.dot_general(
            features, grad_proj, (((0,), (0,)), ((), ())), preferred_element_type=jnp.float32
        ),
        "dp",
        scatter_dimension=0,
        tiled=True,
    )
    along_pose = jnp.sum(unit_pose * grad_pose, axis=1, keepdims=True)
    pose_grad = ((grad_pose - unit_pose * along_pose) / norm_pose).astype(jnp.bfloat16)
    return (pose_grad, head_grad, loss_terms, scale_grad)


def solution(mesh):
    return jax.shard_map(
        local,
        mesh=mesh,
        in_specs=(P("dp", None), P("dp", None), P("dp", None), P(), P(), P()),
        out_specs=(P("dp", None), P("dp", None), P(), P()),
        check_vma=False,
    )
```

profile of v0, /device:TPU:1, one launch (start us, length us, event | category | flops | bytes accessed | tf_op | source)
XLA Modules:
  0.0 445.1 jit_solution(4143440137941111830)
XLA Ops:
  7.2 0.7 all-gather.3.cloned.1.call-update
  8.0 1.1 fusion
  9.1 1.1 fusion.30
  10.1 16.6 %collective-permute-start = (bf16[128,1024]{1,0:T(8,128)(2,1)S(1)}, bf16[128,1024]{1,0:T(8,128)(2,1)S(1)}, u32[]{:S(2)}, u32[]{:S(2)}) collective-permute-start(bf16[128,1024]{1,0:T(8,128)(2,1)S(1)} %fusion.30), channel_id=1, source_target_pairs={{0,510},{1,511},{2,0},{3,1},{4,2},{5,3},{6,4},{7,5},{8,6},{9,7},{1... | collective-permute-start | bytes 786440 | tf_op jit(solution)/shard_map/ppermute | solution.py:14
  26.7 5.0 %collective-permute-done = bf16[128,1024]{1,0:T(8,128)(2,1)S(1)} collective-permute-done((bf16[128,1024]{1,0:T(8,128)(2,1)S(1)}, bf16[128,1024]{1,0:T(8,128)(2,1)S(1)}, u32[]{:S(2)}, u32[]{:S(2)}) %collective-permute-start) | collective-permute-done | bytes 262176 | tf_op jit(solution)/shard_map/ppermute | solution.py:14
  31.7 1.9 collective-permute-start.2
  33.6 3.3 collective-permute-done.2
  36.9 4.4 collective-permute-start.4
  41.3 8.0 %collective-permute-done.4 = bf16[128,1024]{1,0:T(8,128)(2,1)S(1)} collective-permute-done((bf16[128,1024]{1,0:T(8,128)(2,1)S(1)}, bf16[128,1024]{1,0:T(8,128)(2,1)S(1)}, u32[]{:S(2)}, u32[]{:S(2)}) %collective-permute-start.4) | collective-permute-done | bytes 262176 | tf_op jit(solution)/shard_map/ppermute | solution.py:14
  49.3 1.9 collective-permute-start.6
  52.6 0.9 fusion.47
  53.5 8.9 %collective-permute-done.6 = bf16[128,1024]{1,0:T(8,128)(2,1)S(1)} collective-permute-done((bf16[128,1024]{1,0:T(8,128)(2,1)S(1)}, bf16[128,1024]{1,0:T(8,128)(2,1)S(1)}, u32[]{:S(2)}, u32[]{:S(2)}) %collective-permute-start.6) | collective-permute-done | bytes 262176 | tf_op jit(solution)/shard_map/ppermute | solution.py:14
  62.4 1.9 collective-permute-start.8
  64.3 69.1 %all-gather.3.cloned.1.call-done = bf16[512,2,1024]{2,1,0:T(2,128)(2,1)} async-done(((bf16[1,2,1024]{2,1,0:T(2,128)(2,1)}), bf16[512,2,1024]{2,1,0:T(2,128)(2,1)}) %all-gather.3.cloned.1.call-update) | async-done | bytes 2097168 | tf_op jit(solution)/shard_map/all_gather | solution.py:49
  133.4 2.7 reshape.29
  136.2 0.5 multiply_reduce_fusion.2
  136.9 0.2 fusion.48
  137.3 0.2 fusion.50
  137.6 1.2 fusion.51
  138.8 1.2 fusion.18
  140.0 0.3 fusion.24
  140.3 3.2 collective-permute-start.1
  143.5 0.3 fusion.23
  143.8 0.3 convolution_add_fusion.3
  144.1 0.3 convolution_add_fusion.2
  144.3 0.3 convolution_add_fusion.1
  144.6 1.3 multiply_reduce_fusion
  145.9 2.8 convolution_bitcast_fusion
  148.8 0.8 collective-permute-done.1
  149.6 0.3 convolution_add_fusion.4
  149.9 4.4 collective-permute-start.3
  154.3 0.3 fusion.25
  154.7 6.4 %collective-permute-done.3 = f32[128,1024]{1,0:T(8,128)S(1)} collective-permute-done((f32[128,1024]{1,0:T(8,128)S(1)}, f32[128,1024]{1,0:T(8,128)S(1)}, u32[]{:S(2)}, u32[]{:S(2)}) %collective-permute-start.3) | collective-permute-done | bytes 524320 | tf_op jit(solution)/shard_map/ppermute | solution.py:14
  161.1 4.4 collective-permute-start.5
  165.5 0.3 fusion.26
  165.8 11.5 %collective-permute-done.5 = f32[128,1024]{1,0:T(8,128)S(1)} collective-permute-done((f32[128,1024]{1,0:T(8,128)S(1)}, f32[128,1024]{1,0:T(8,128)S(1)}, u32[]{:S(2)}, u32[]{:S(2)}) %collective-permute-start.5) | collective-permute-done | bytes 524320 | tf_op jit(solution)/shard_map/ppermute | solution.py:14
  177.4 2.1 collective-permute-start.7
  179.5 0.3 fusion.27
  179.8 14.9 %collective-permute-done.7 = f32[128,1024]{1,0:T(8,128)S(1)} collective-permute-done((f32[128,1024]{1,0:T(8,128)S(1)}, f32[128,1024]{1,0:T(8,128)S(1)}, u32[]{:S(2)}, u32[]{:S(2)}) %collective-permute-start.7) | collective-permute-done | bytes 524320 | tf_op jit(solution)/shard_map/ppermute | solution.py:14
  194.7 14.4 %collective-permute-start.9 = (f32[128,1024]{1,0:T(8,128)S(1)}, f32[128,1024]{1,0:T(8,128)S(1)}, u32[]{:S(2)}, u32[]{:S(2)}) collective-permute-start(f32[128,1024]{1,0:T(8,128)S(1)} %add.185), channel_id=1, source_target_pairs={{0,510},{1,511},{2,0},{3,1},{4,2},{5,3},{6,4},{7,5},{8,6},{9,7},{1... | collective-permute-start | bytes 1572872 | tf_op jit(solution)/shard_map/ppermute | solution.py:14
  209.1 9.4 %maximum_add_fusion.1 = f32[3]{0:T(128)S(1)} fusion(f32[1]{0:T(128)} %bitcast.18, f32[1]{0:T(128)} %bitcast.17, f32[1]{0:T(128)} %bitcast.16, f32[1]{0:T(128)} %bitcast.15, f32[1]{0:T(128)} %bitcast.14, f32[1]{0:T(128)} %bitcast.13, f32[1]{0:T(128)} %bitcast.12, f32[1]{0:T(128)} %bitcast.11, f32[1]{0:T(128)} %bitcast.10, f32[1]{0:T(128)} %bitcast.9, ...), kind=kLoop, calls=%fused_computation.75 | loop fusion | flops 42 | bytes 72 | tf_op jit(solution)/shard_map/add | solution.py:79
  218.5 94.7 %psum.7 = f32[3]{0:T(128)S(1)} all-reduce(f32[3]{0:T(128)S(1)} %maximum_add_fusion.1), channel_id=1, replica_groups=mesh['dp'=512] {'dp'}, use_global_device_ids=true, to_apply=%region_20.21 | all-reduce | flops 3 | bytes 24 | tf_op jit(solution)/shard_map/psum | solution.py:85
  313.2 0.6 slice.7
  314.4 0.5 slice_multiply_fusion
  314.9 119.1 %all-reduce.3.cloned.1.call-done = f32[1024,1024]{0,1:T(8,128)} async-done(((f32[1024,1024]{0,1:T(8,128)}), f32[1024,1024]{0,1:T(8,128)}) %all-reduce.3.cloned.1.call-update) | async-done | bytes 4194320
  434.0 1.2 constant_dynamic-slice_fusion
  435.3 0.8 copy.11
  436.3 0.9 divide_convert_fusion.1
  (17 shorter events, 0.9 us)
Async XLA Ops:
  7.2 129.0 %copy-start = (bf16[128,1024]{1,0:T(8,128)(2,1)S(1)}, bf16[128,1024]{1,0:T(8,128)(2,1)}, u32[]{:S(2)}) copy-start(bf16[128,1024]{1,0:T(8,128)(2,1)} %param.6) | copy-start | bytes 786436
  7.2 126.2 %all-gather.3.cloned.1.call-start = ((), (), s32[]{:S(2)}) async-start(), calls=%async_computation | async-start | bytes 2101248 | tf_op jit(solution)/shard_map/all_gather | solution.py:49
  7.9 426.1 %all-reduce.3.cloned.1.call-start = ((), (), s32[]{:S(2)}) async-start(), calls=%async_computation.1 | async-start | bytes 8388608
  10.1 21.6 %collective-permute-start = (bf16[128,1024]{1,0:T(8,128)(2,1)S(1)}, bf16[128,1024]{1,0:T(8,128)(2,1)S(1)}, u32[]{:S(2)}, u32[]{:S(2)}) collective-permute-start(bf16[128,1024]{1,0:T(8,128)(2,1)S(1)} %fusion.30), channel_id=1, source_target_pairs={{0,510},{1,511},{2,0},{3,1},{4,2},{5,3},{6,4},{7,5},{8,6},{9,7},{1... | collective-permute-start | bytes 786440 | tf_op jit(solution)/shard_map/ppermute | solution.py:14
  31.7 5.2 %collective-permute-start.2 = (bf16[128,1024]{1,0:T(8,128)(2,1)S(1)}, bf16[128,1024]{1,0:T(8,128)(2,1)S(1)}, u32[]{:S(2)}, u32[]{:S(2)}) collective-permute-start(bf16[128,1024]{1,0:T(8,128)(2,1)S(1)} %collective-permute-done), channel_id=1, source_target_pairs={{0,1},{1,2},{2,3},{3,4},{4,5},{5,6},{6,7},{7,8},{8,9},{9,10},{10,1... | collective-permute-start | bytes 786440 | tf_op jit(solution)/shard_map/ppermute | solution.py:14
  36.9 12.4 %collective-permute-start.4 = (bf16[128,1024]{1,0:T(8,128)(2,1)S(1)}, bf16[128,1024]{1,0:T(8,128)(2,1)S(1)}, u32[]{:S(2)}, u32[]{:S(2)}) collective-permute-start(bf16[128,1024]{1,0:T(8,128)(2,1)S(1)} %collective-permute-done.2), channel_id=1, source_target_pairs={{0,1},{1,2},{2,3},{3,4},{4,5},{5,6},{6,7},{7,8},{8,9},{9,10},{10,1... | collective-permute-start | bytes 786440 | tf_op jit(solution)/shard_map/ppermute | solution.py:14
  49.3 13.1 %collective-permute-start.6 = (bf16[128,1024]{1,0:T(8,128)(2,1)S(1)}, bf16[128,1024]{1,0:T(8,128)(2,1)S(1)}, u32[]{:S(2)}, u32[]{:S(2)}) collective-permute-start(bf16[128,1024]{1,0:T(8,128)(2,1)S(1)} %collective-permute-done.4), channel_id=1, source_target_pairs={{0,1},{1,2},{2,3},{3,4},{4,5},{5,6},{6,7},{7,8},{8,9},{9,10},{10,1... | collective-permute-start | bytes 786440 | tf_op jit(solution)/shard_map/ppermute | solution.py:14
  62.4 75.2 %collective-permute-start.8 = (bf16[128,1024]{1,0:T(8,128)(2,1)S(1)}, bf16[128,1024]{1,0:T(8,128)(2,1)}, u32[]{:S(2)}, u32[]{:S(2)}) collective-permute-start(bf16[128,1024]{1,0:T(8,128)(2,1)S(1)} %collective-permute-done.6), channel_id=1, source_target_pairs={{0,1},{1,2},{2,3},{3,4},{4,5},{5,6},{6,7},{7,8},{8,9},{9,10},{10,1... | collective-permute-start | bytes 786440 | tf_op jit(solution)/shard_map/ppermute | solution.py:14
  140.3 9.3 %collective-permute-start.1 = (f32[128,1024]{1,0:T(8,128)S(1)}, f32[128,1024]{1,0:T(8,128)S(1)}, u32[]{:S(2)}, u32[]{:S(2)}) collective-permute-start(f32[128,1024]{1,0:T(8,128)S(1)} %fusion.24), channel_id=1, source_target_pairs={{0,1},{1,2},{2,3},{3,4},{4,5},{5,6},{6,7},{7,8},{8,9},{9,10},{10,1... | collective-permute-start | bytes 1572872 | tf_op jit(solution)/shard_map/ppermute | solution.py:14
  149.9 11.1 %collective-permute-start.3 = (f32[128,1024]{1,0:T(8,128)S(1)}, f32[128,1024]{1,0:T(8,128)S(1)}, u32[]{:S(2)}, u32[]{:S(2)}) collective-permute-start(f32[128,1024]{1,0:T(8,128)S(1)} %convolution_add_fusion.4), channel_id=1, source_target_pairs={{0,1},{1,2},{2,3},{3,4},{4,5},{5,6},{6,7},{7,8},{8,9},{9,10},{10,1... | collective-permute-start | bytes 1572872 | tf_op jit(solution)/shard_map/ppermute | solution.py:14
  161.1 16.3 %collective-permute-start.5 = (f32[128,1024]{1,0:T(8,128)S(1)}, f32[128,1024]{1,0:T(8,128)S(1)}, u32[]{:S(2)}, u32[]{:S(2)}) collective-permute-start(f32[128,1024]{1,0:T(8,128)S(1)} %add.173), channel_id=1, source_target_pairs={{0,1},{1,2},{2,3},{3,4},{4,5},{5,6},{6,7},{7,8},{8,9},{9,10},{10,1... | collective-permute-start | bytes 1572872 | tf_op jit(solution)/shard_map/ppermute | solution.py:14
  177.4 258.7 %copy-start.1 = (bf16[128,1024]{1,0:T(8,128)(2,1)S(1)}, bf16[128,1024]{1,0:T(8,128)(2,1)}, u32[]{:S(2)}) copy-start(bf16[128,1024]{1,0:T(8,128)(2,1)} %param.8) | copy-start | bytes 786436
  177.4 17.2 %collective-permute-start.7 = (f32[128,1024]{1,0:T(8,128)S(1)}, f32[128,1024]{1,0:T(8,128)S(1)}, u32[]{:S(2)}, u32[]{:S(2)}) collective-permute-start(f32[128,1024]{1,0:T(8,128)S(1)} %add.179), channel_id=1, source_target_pairs={{0,1},{1,2},{2,3},{3,4},{4,5},{5,6},{6,7},{7,8},{8,9},{9,10},{10,1... | collective-permute-start | bytes 1572872 | tf_op jit(solution)/shard_map/ppermute | solution.py:14
  194.7 241.3 %collective-permute-start.9 = (f32[128,1024]{1,0:T(8,128)S(1)}, f32[128,1024]{1,0:T(8,128)S(1)}, u32[]{:S(2)}, u32[]{:S(2)}) collective-permute-start(f32[128,1024]{1,0:T(8,128)S(1)} %add.185), channel_id=1, source_target_pairs={{0,510},{1,511},{2,0},{3,1},{4,2},{5,3},{6,4},{7,5},{8,6},{9,7},{1... | collective-permute-start | bytes 1572872 | tf_op jit(solution)/shard_map/ppermute | solution.py:14
Sparse Core Ops, SparseCore 0:
  12.2 121.1 all-gather.2
  148.9 285.0 all-reduce.2
where the time goes:
time: 447 us; the launch traced here: 445 us
  waiting for transfers between devices  248 us (55%)
  blocking collectives  94.7 us (21%)
  starting transfers between devices  55.2 us (12%)
  between operations  17.5 us (4%)
  other arithmetic  13.5 us (3%)
  matrix products  10.4 us (2%)
  local copies, waits for them, and re-layouts  6.29 us (1%)
    unnamed x3, waiting for transfers between devices  120 us
    psum x1, blocking collectives, local(): summed = lax.psum(totals, 'dp')  94.7 us
    all_gather x1, waiting for transfers between devices, local(): head_full = lax.all_gather(head_rows, 'dp', axis=0, tiled=True)  69.1 us
    ppermute x10, waiting for transfers between devices, passed_along(): lax.ppermute(array, axis, [(i, (i + by) % length) for i in range(length)])  58.7 us
    ppermute x10, starting transfers between devices, passed_along(): lax.ppermute(array, axis, [(i, (i + by) % length) for i in range(length)])  55.1 us
    add x1, other arithmetic, local(): totals = totals + partial_value  9.4 us
  transfers between devices with their start and end apart: 12, of which 10 were waited for; matrix products, arithmetic and copies ran while one was open for 6% of the time, Pallas kernels for 0%

commit v1 on v0

v1 whole, which is shorter than its diff:
```python
import functools

import jax
import jax.numpy as jnp
from jax import lax
from jax.experimental import pallas as pl
from jax.experimental.pallas import tpu as pltpu
from jax.sharding import PartitionSpec as P

REACH = 2
WINDOW = 2 * REACH + 1
EPS = 1e-06
ROWS = 128
COLS = 128
GROUP = 8
SIDE = 8
CELLS = SIDE * SIDE
COUNT = GROUP * CELLS
BATCH = ROWS * COUNT
WIDTH = GROUP * COLS
TILE = 16
HALF = ROWS // 2

F32 = jnp.float32
BF16 = jnp.bfloat16


def remote(src, dst, send_sem, recv_sem, device):
    return pltpu.make_async_remote_copy(
        src_ref=src,
        dst_ref=dst,
        send_sem=send_sem,
        recv_sem=recv_sem,
        device_id=(device,),
        device_id_type=pl.DeviceIdType.MESH,
    )


def dot(left, right, dims):
    return lax.dot_general(left, right, (dims, ((), ())), preferred_element_type=F32)


def softplus_parts(logits):
    tail = jnp.exp(-jnp.abs(logits))
    share = 1.0 / (1.0 + tail)
    sigmoid = jnp.where(logits >= 0, share, tail * share)
    return jnp.log1p(tail), sigmoid


def kernel(
    feat_hbm, head_ref, pose_hbm, ids_ref, scale_ref, bias_ref,
    pose_grad_ref, head_grad_ref, loss_ref, scale_grad_ref,
    feats, feats_t, pose_raw, poses, embs, piece_src, piece, tile_f32, head,
    proj_src, proj, unit, inv_pose, gp_src, gp, part_src, part, fin_src, fin,
    tot_src, tot_group, tot_z_src, tot_z, tot_y_src, tot_y,
    local_sem, piece_s, piece_r, feat_s, feat_r, head_s, head_r, pose_s, pose_r, emb_s, emb_r,
    proj_s, proj_r, gp_s, gp_r, part_s, part_r, fin_s, fin_r, tot_s, tot_r,
):
    me = lax.axis_index("dp")
    slot = lax.rem(me, GROUP)
    cell = me // GROUP
    y = cell // SIDE
    z = lax.rem(cell, SIDE)
    core = lax.rem(me, 2)
    base = me - slot
    sibling = me + 1 - 2 * core

    def mate_slot(step):
        return lax.rem(slot + step, GROUP)

    def plane_cell(step_y, step_z):
        return lax.rem(y + step_y, SIDE) * SIDE + lax.rem(z + step_z, SIDE)

    def ring(step):
        return lax.rem(me + step + COUNT, COUNT)

    load_feat = pltpu.make_async_copy(feat_hbm, feats.at[slot], local_sem.at[0])
    load_pose = pltpu.make_async_copy(pose_hbm, pose_raw, local_sem.at[1])
    load_pose.start()
    load_feat.start()

    barrier = pltpu.get_barrier_semaphore()

    def greet(device):
        pl.semaphore_signal(barrier, inc=1, device_id=(device,), device_id_type=pl.DeviceIdType.MESH)

    for step in range(1, GROUP):
        greet(base + mate_slot(step))
    for step in (-2, -1, 1, 2):
        greet(ring(step))

    @pl.loop(1, CELLS)
    def _(step):
        greet(plane_cell(step // SIDE, lax.rem(step, SIDE)) * GROUP + slot)

    rows = head_ref[...].astype(F32)
    piece_src[...] = jnp.zeros_like(piece_src)
    for number in range(GROUP):
        piece_src[number, 0:2, :] = rows[:, number * COLS : (number + 1) * COLS]
    piece[slot] = piece_src[slot]

    pl.semaphore_wait(barrier, GROUP - 1 + 4 + CELLS - 1)

    piece_copies = []
    for step in (4, 5, 3, 2, 6, 7, 1):
        copy = remote(
            piece_src.at[mate_slot(step)], piece.at[slot], piece_s.at[step], piece_r.at[step], base + mate_slot(step)
        )
        copy.start()
        piece_copies.append(copy)

    load_feat.wait()
    right = base + mate_slot(2)
    left = base + mate_slot(6)

    def half(of_slot, number):
        return feats.at[of_slot, pl.ds(number * HALF, HALF), :]

    def send_half(of_slot, number, device, sem):
        copy = remote(half(of_slot, number), half(of_slot, number), feat_s.at[sem], feat_r.at[sem], device)
        copy.start()
        return copy

    def send_block(of_slot, sem):
        copy = remote(feats.at[of_slot], feats.at[of_slot], feat_s.at[sem], feat_r.at[sem], sibling)
        copy.start()
        return copy

    right_a = send_half(slot, 0, right, 0)
    left_b = send_half(slot, 1, left, 1)
    right_b = send_half(slot, 1, right, 2)
    left_a = send_half(slot, 0, left, 3)
    block_own = send_block(slot, 6)

    for copy in piece_copies:
        copy.wait_recv()
    for number in range(GROUP):
        tile_f32[2 * number : 2 * number + 2, :] = piece[number, 0:2, :]
    head[cell] = tile_f32[...].astype(BF16)

    @pl.loop(1, CELLS)
    def _(step):
        device = plane_cell(step // SIDE, lax.rem(step, SIDE)) * GROUP + slot
        remote(head.at[cell], head.at[cell], head_s, head_r, device).start()

    load_pose.wait()
    raw = pose_raw[...].astype(F32)
    inv_p = 1.0 / jnp.sqrt(jnp.sum(raw * raw, axis=1, keepdims=True) + EPS)
    inv_pose[...] = jnp.broadcast_to(inv_p, (ROWS, COLS))
    poses[REACH] = (raw * inv_p).astype(BF16)

    right_a.wait_recv()
    right_a2 = send_half(mate_slot(6), 0, right, 4)
    left_b.wait_recv()
    left_b2 = send_half(mate_slot(2), 1, left, 5)
    right_b.wait_recv()
    block_left = send_block(mate_slot(6), 7)
    left_a.wait_recv()
    block_right = send_block(mate_slot(2), 8)
    right_a2.wait_recv()
    left_b2.wait_recv()
    block_far = send_block(mate_slot(4), 9)

    def exchange(blocks, sems, semr):
        ahead = remote(blocks.at[REACH], blocks.at[0], sems.at[0], semr.at[0], ring(2))
        behind = remote(blocks.at[REACH], blocks.at[4], sems.at[1], semr.at[4], ring(-2))
        beside = remote(
            blocks.at[REACH], blocks.at[1 + 2 * core], sems.at[2], semr.at[1 + 2 * core], sibling
        )
        passed = remote(
            blocks.at[4 - 4 * core], blocks.at[3 - 2 * core], sems.at[3], semr.at[3 - 2 * core], sibling
        )
        ahead.start()
        behind.start()
        beside.start()

        def forward():
            ahead.wait_recv()
            behind.wait_recv()
            passed.start()

        def finish():
            remote(blocks.at[REACH], blocks.at[1], sems.at[2], semr.at[1], sibling).wait_recv()
            remote(blocks.at[REACH], blocks.at[3], sems.at[3], semr.at[3], sibling).wait_recv()

        def drain():
            ahead.wait_send()
            behind.wait_send()
            beside.wait_send()
            passed.wait_send()

        return forward, finish, drain

    pose_forward, pose_finish, pose_drain = exchange(poses, pose_s, pose_r)

    for copy in (block_own, block_left, block_right, block_far):
        copy.wait_recv()
    for number in range(GROUP):
        feats_t[:, number * ROWS : (number + 1) * ROWS] = feats[number].T

    pltpu.make_async_copy(head.at[pl.ds(0, CELLS - 1)], head.at[pl.ds(0, CELLS - 1)], head_r).wait()
    head_cols = head[...].reshape(WIDTH, COLS)
    proj_copies = []
    for step in (4, 5, 3, 2, 6, 7, 1):
        to = mate_slot(step)
        proj_src[step] = dot(feats[to], head_cols, ((1,), (0,)))
        copy = remote(proj_src.at[step], proj.at[slot], proj_s.at[step], proj_r.at[step], base + to)
        copy.start()
        proj_copies.append(copy)
    proj[slot] = dot(feats[slot], head_cols, ((1,), (0,)))

    pose_forward()
    pose_finish()
    for copy in proj_copies:
        copy.wait_recv()

    square = jnp.zeros((ROWS, COLS), F32)
    for number in range(GROUP):
        value = proj[number]
        square = square + value * value
    inv_i = 1.0 / jnp.sqrt(jnp.sum(square, axis=1, keepdims=True) + EPS)
    for number in range(GROUP):
        value = proj[number] * inv_i
        unit[:, number * COLS : (number + 1) * COLS] = value
        embs[REACH, :, number * COLS : (number + 1) * COLS] = value.astype(BF16)

    scale = scale_ref[0]
    bias = bias_ref[0]

    def ids_of(step):
        return ids_ref[pl.ds(ring(step), 1), :]

    own_ids = jnp.broadcast_to(ids_of(0), (ROWS, ROWS)).T

    def window_terms(left_emb, blocks, with_totals):
        weights = []
        totals = [jnp.zeros((1, COLS), F32) for _ in range(3)]
        for number in range(WINDOW):
            inner = dot(left_emb, blocks[number], ((1,), (1,)))
            logits = scale * inner + bias
            matched = own_ids == ids_of(number - REACH)
            tail, sigmoid = softplus_parts(logits)
            gradient = sigmoid - matched.astype(F32)
            weights.append((scale * gradient).astype(BF16))
            if with_totals:
                signed = jnp.where(matched, logits, -logits)
                loss = tail - jnp.minimum(signed, 0.0)
                for place, term in enumerate((loss, gradient, gradient * inner)):
                    totals[place] = totals[place] + jnp.sum(term, axis=0, keepdims=True)
        return jnp.concatenate(weights, axis=1), totals

    weight, totals = window_terms(embs[REACH], poses, True)
    tot_src[...] = jnp.zeros_like(tot_src)
    for place in range(3):
        tot_src[place : place + 1, :] = totals[place]
    tot_copies = []
    for step in range(1, GROUP):
        copy = remote(tot_src, tot_group.at[slot], tot_s.at[step], tot_r.at[step], base + mate_slot(step))
        copy.start()
        tot_copies.append(copy)
    tot_group[slot] = tot_src[...]

    grad_img = dot(weight, poses[...].reshape(WINDOW * ROWS, WIDTH), ((1,), (0,)))
    unit_img = unit[...]
    along = jnp.sum(unit_img * grad_img, axis=1, keepdims=True)
    grad_proj = ((grad_img - unit_img * along) * inv_i).astype(BF16)
    for number in range(GROUP):
        gp_src[number] = grad_proj[:, number * COLS : (number + 1) * COLS]
    gp_copies = []
    for step in (4, 5, 3, 2, 6, 7, 1):
        to = mate_slot(step)
        copy = remote(gp_src.at[to], gp.at[slot], gp_s.at[step], gp_r.at[step], base + to)
        copy.start()
        gp_copies.append(copy)
    gp[slot] = gp_src[slot]

    for copy in tot_copies:
        copy.wait_recv()
    group_sum = tot_group[0]
    for number in range(1, GROUP):
        group_sum = group_sum + tot_group[number]
    tot_z_src[...] = group_sum
    tot_z[z] = group_sum
    z_copies = []
    for step in range(1, SIDE):
        copy = remote(
            tot_z_src, tot_z.at[z], tot_s.at[8 + step], tot_r.at[8 + step], plane_cell(0, step) * GROUP + slot
        )
        copy.start()
        z_copies.append(copy)

    for copy in gp_copies:
        copy.wait_recv()

    @pl.loop(0, SIDE)
    def _(step_y):
        row = lax.rem(y + step_y, SIDE)
        start = pl.multiple_of(row * (SIDE * TILE), SIDE * TILE)
        value = dot(feats_t[pl.ds(start, SIDE * TILE), :], gp[...].reshape(GROUP * ROWS, COLS), ((1,), (0,)))
        part_src[pl.ds(row * SIDE, SIDE)] = value.astype(BF16).reshape(SIDE, TILE, COLS)

        @pl.loop(0, SIDE)
        def _(step_z):
            to = plane_cell(step_y, step_z)

            @pl.when(step_y + step_z > 0)
            def _():
                remote(part_src.at[to], part.at[cell], part_s, part_r, to * GROUP + slot).start()

    part[cell] = part_src[cell]

    emb_forward, emb_finish, emb_drain = exchange(embs, emb_s, emb_r)

    for copy in z_copies:
        copy.wait_recv()
    z_sum = tot_z[0]
    for number in range(1, SIDE):
        z_sum = z_sum + tot_z[number]
    tot_y_src[...] = z_sum
    tot_y[y] = z_sum
    y_copies = []
    for step in range(1, SIDE):
        copy = remote(
            tot_y_src, tot_y.at[y], tot_s.at[16 + step], tot_r.at[16 + step], plane_cell(step, 0) * GROUP + slot
        )
        copy.start()
        y_copies.append(copy)

    emb_forward()
    emb_finish()
    pose_weight, _ = window_terms(poses[REACH], embs, False)
    grad_pose = dot(pose_weight, embs[...].reshape(WINDOW * ROWS, WIDTH), ((1,), (0,)))
    inv_q = inv_pose[:, 0:1]
    unit_pose = pose_raw[...].astype(F32) * inv_q
    along_pose = jnp.sum(unit_pose * grad_pose, axis=1, keepdims=True)
    pose_grad_ref[...] = ((grad_pose - unit_pose * along_pose) * inv_q).astype(BF16)

    pltpu.make_async_copy(part.at[pl.ds(0, CELLS - 1)], part.at[pl.ds(0, CELLS - 1)], part_r).wait()
    summed = jnp.sum(part[...].astype(F32), axis=0)
    fin_src[...] = jnp.zeros_like(fin_src)
    for number in range(GROUP):
        fin_src[number, 0:2, :] = summed[2 * number : 2 * number + 2, :]
    fin_copies = []
    for step in (4, 5, 3, 2, 6, 7, 1):
        to = mate_slot(step)
        copy = remote(fin_src.at[to], fin.at[slot], fin_s.at[step], fin_r.at[step], base + to)
        copy.start()
        fin_copies.append(copy)
    fin[slot] = fin_src[slot]

    for copy in y_copies:
        copy.wait_recv()
    y_sum = tot_y[0]
    for number in range(1, SIDE):
        y_sum = y_sum + tot_y[number]
    y_sum = y_sum / BATCH
    loss_ref[0] = jnp.sum(y_sum[0:1, :])
    loss_ref[1] = jnp.sum(y_sum[1:2, :])
    scale_grad_ref[0] = jnp.sum(y_sum[2:3, :])

    for copy in fin_copies:
        copy.wait_recv()
    for number in range(GROUP):
        head_grad_ref[:, number * COLS : (number + 1) * COLS] = fin[number, 0:2, :]

    for copy in piece_copies + proj_copies + gp_copies + fin_copies + tot_copies + z_copies + y_copies:
        copy.wait_send()
    for copy in (right_a, left_b, right_b, left_a, right_a2, left_b2, block_own, block_left, block_right, block_far):
        copy.wait_send()
    pose_drain()
    emb_drain()
    pltpu.make_async_copy(head.at[pl.ds(0, CELLS - 1)], head.at[pl.ds(0, CELLS - 1)], head_s).wait()
    pltpu.make_async_copy(part_src.at[pl.ds(0, CELLS - 1)], part_src.at[pl.ds(0, CELLS - 1)], part_s).wait()


def local(features, head_rows, poses, match_ids, logit_scale, logit_bias):
    vmem = pl.BlockSpec(memory_space=pltpu.VMEM)
    smem = pl.BlockSpec(memory_space=pltpu.SMEM)
    hbm = pl.BlockSpec(memory_space=pl.ANY)
    dma = pltpu.SemaphoreType.DMA
    block = (ROWS, WIDTH)
    square = (GROUP, ROWS, COLS)
    return pl.pallas_call(
        kernel,
        name="contrastive",
        out_shape=(
            jax.ShapeDtypeStruct(block, BF16),
            jax.ShapeDtypeStruct((2, WIDTH), F32),
            jax.ShapeDtypeStruct((2,), F32),
            jax.ShapeDtypeStruct((1,), F32),
        ),
        in_specs=[hbm, vmem, hbm, vmem, smem, smem],
        out_specs=(vmem, vmem, smem, smem),
        scratch_shapes=[
            pltpu.VMEM((GROUP,) + block, BF16),
            pltpu.VMEM((WIDTH, GROUP * ROWS), BF16),
            pltpu.VMEM(block, BF16),
            pltpu.VMEM((WINDOW,) + block, BF16),
            pltpu.VMEM((WINDOW,) + block, BF16),
            pltpu.VMEM((GROUP, 8, COLS), F32),
            pltpu.VMEM((GROUP, 8, COLS), F32),
            pltpu.VMEM((TILE, COLS), F32),
            pltpu.VMEM((CELLS, TILE, COLS), BF16),
            pltpu.VMEM(square, F32),
            pltpu.VMEM(square, F32),
            pltpu.VMEM(block, F32),
            pltpu.VMEM((ROWS, COLS), F32),
            pltpu.VMEM(square, BF16),
            pltpu.VMEM(square, BF16),
            pltpu.VMEM((CELLS, TILE, COLS), BF16),
            pltpu.VMEM((CELLS, TILE, COLS), BF16),
            pltpu.VMEM((GROUP, 8, COLS), F32),
            pltpu.VMEM((GROUP, 8, COLS), F32),
            pltpu.VMEM((8, COLS), F32),
            pltpu.VMEM((GROUP, 8, COLS), F32),
            pltpu.VMEM((8, COLS), F32),
            pltpu.VMEM((SIDE, 8, COLS), F32),
            pltpu.VMEM((8, COLS), F32),
            pltpu.VMEM((SIDE, 8, COLS), F32),
            dma((2,)),
            dma((GROUP,)), dma((GROUP,)),
            dma((10,)), dma((10,)),
            dma, dma,
            dma((4,)), dma((WINDOW,)),
            dma((4,)), dma((WINDOW,)),
            dma((GROUP,)), dma((GROUP,)),
            dma((GROUP,)), dma((GROUP,)),
            dma, dma,
            dma((GROUP,)), dma((GROUP,)),
            dma((24,)), dma((24,)),
        ],
        compiler_params=pltpu.CompilerParams(
            collective_id=0, has_side_effects=True, vmem_limit_bytes=48 * 1024 * 1024
        ),
    )(features, head_rows, poses, match_ids.reshape(COUNT, ROWS), logit_scale, logit_bias)


def solution(mesh):
    return jax.shard_map(
        local,
        mesh=mesh,
        in_specs=(P("dp", None), P("dp", None), P("dp", None), P(), P(), P()),
        out_specs=(P("dp", None), P("dp", None), P(), P()),
        check_vma=False,
    )
```

time: 447 us -> 80.6 us (0.18)
  waiting for transfers between devices: 248 us -> 0 us
  blocking collectives: 94.7 us -> 0 us
  Pallas kernels: 0 us -> 72 us
  starting transfers between devices: 55.2 us -> 0 us
  between operations: 17.5 us -> 3.72 us
  other arithmetic: 13.5 us -> 0 us
  matrix products: 10.4 us -> 0 us
    unnamed x3 -> x0, waiting for transfers between devices: 120 us -> none
    psum x1 -> x0, blocking collectives: 94.7 us -> none  [local(): summed = lax.psum(totals, 'dp')]
    pallas_call x0 -> x1, Pallas kernels: none -> 72 us  [local(): pl.pallas_call(kernel, name='contrastive', out_shape=(jax.ShapeDtypeStruc...]
    all_gather x1 -> x0, waiting for transfers between devices: 69.1 us -> none  [local(): head_full = lax.all_gather(head_rows, 'dp', axis=0, tiled=True)]
    ppermute x10 -> x0, waiting for transfers between devices: 58.7 us -> none  [passed_along(): lax.ppermute(array, axis, [(i, (i + by) % length) for i in range(length)])]
    ppermute x10 -> x0, starting transfers between devices: 55.1 us -> none  [passed_along(): lax.ppermute(array, axis, [(i, (i + by) % length) for i in range(length)])]
    dot_general x17 -> x0, matrix products: 10.4 us -> none  [the longest x5 3.09 us: tile_terms(): lax.dot_general(left_emb, right_emb, (((1,), (1,)), ((), ())), preferred_...]
    add x4 -> x0, other arithmetic: 9.57 us -> none  [the longest x1 9.4 us: local(): totals = totals + partial_value]
  transfers between devices with their start and end apart: 12 -> 0, of which waited for: 10 -> 0; matrix products, arithmetic and copies ran while one was open for 6% -> 0% of each run, Pallas kernels for 0% -> 0%
where the time goes in v1:
time: 80.6 us; the launch traced here: 80.3 us
  Pallas kernels  72 us (89%)
  local copies, waits for them, and re-layouts  4.66 us (6%)
  between operations  3.72 us (5%)
    pallas_call x1, Pallas kernels, local(): pl.pallas_call(kernel, name='contrastive', out_shape=(jax.ShapeDtypeStruc...  72 us
    unnamed x11, local copies, waits for them, and re-layouts  4.66 us

profile of v1, /device:TPU:1, one launch (start us, length us, event | category | flops | bytes accessed | tf_op | source)
XLA Modules:
  0.0 80.3 jit_solution(18214070045244239182)
XLA Ops:
  0.6 0.0 copy-start.3
  1.9 0.0 copy-done.3
  2.0 0.0 copy-start
  2.0 0.9 %copy-done = bf16[128,1024]{1,0:T(8,128)(2,1)S(1)} copy-done((bf16[128,1024]{1,0:T(8,128)(2,1)S(1)}, bf16[128,1024]{1,0:T(8,128)(2,1)}, u32[]{:S(2)}) %copy-start) | copy-done | bytes 262168
  2.9 0.0 copy-start.1
  2.9 0.9 %copy-done.1 = bf16[128,1024]{1,0:T(8,128)(2,1)S(1)} copy-done((bf16[128,1024]{1,0:T(8,128)(2,1)S(1)}, bf16[128,1024]{1,0:T(8,128)(2,1)}, u32[]{:S(2)}) %copy-start.1) | copy-done | bytes 262168
  3.9 0.0 copy-start.2
  3.9 0.9 %copy-done.2 = s32[65536]{0:T(1024)S(1)} copy-done((s32[65536]{0:T(1024)S(1)}, s32[65536]{0:T(1024)}, u32[]{:S(2)}) %copy-start.2) | copy-done | bytes 262168
  4.8 72.0 %contrastive.1 = (bf16[128,1024]{1,0:T(8,128)(2,1)S(1)}, f32[2,1024]{1,0:T(2,128)S(1)}, f32[2]{0:T(128)S(1)}, f32[1]{0:T(128)}) custom-call(bf16[128,1024]{1,0:T(8,128)(2,1)S(1)} %copy-done, bf16[2,1024]{1,0:T(2,128)(2,1)S(1)} %copy-done.3, bf16[128,1024]{1,0:T(8,128)(2,1)S(1)} %copy-done.1, s32[512,128]{1,0:T(8,128)S(1)} %bitcast.1, f32[1]{0:T(128)S(6)} %copy.14.scale_ref, ...), custom_call_target="tpu_custom_call" | custom-call | tf_op jit(solution)/shard_map/contrastive/pallas_call | solution.py:383
  76.8 0.7 copy.16
  77.5 0.6 copy.17
  78.1 0.5 copy.18
Async XLA Ops:
  0.6 1.3 %copy-start.3 = (bf16[2,1024]{1,0:T(2,128)(2,1)S(1)}, bf16[2,1024]{1,0:T(2,128)(2,1)}, u32[]{:S(2)}) copy-start(bf16[2,1024]{1,0:T(2,128)(2,1)} %head_ref.1) | copy-start | bytes 12292
  2.0 1.0 %copy-start = (bf16[128,1024]{1,0:T(8,128)(2,1)S(1)}, bf16[128,1024]{1,0:T(8,128)(2,1)}, u32[]{:S(2)}) copy-start(bf16[128,1024]{1,0:T(8,128)(2,1)} %feat_hbm.1) | copy-start | bytes 786436
  2.9 0.9 %copy-start.1 = (bf16[128,1024]{1,0:T(8,128)(2,1)S(1)}, bf16[128,1024]{1,0:T(8,128)(2,1)}, u32[]{:S(2)}) copy-start(bf16[128,1024]{1,0:T(8,128)(2,1)} %pose_hbm.1) | copy-start | bytes 786436
  3.9 0.9 %copy-start.2 = (s32[65536]{0:T(1024)S(1)}, s32[65536]{0:T(1024)}, u32[]{:S(2)}) copy-start(s32[65536]{0:T(1024)} %param.9) | copy-start | bytes 786436

commit v2 on v1

v2 whole, which is shorter than its diff:
```python
import jax
import jax.numpy as jnp
from jax import lax
from jax.experimental import pallas as pl
from jax.experimental.pallas import tpu as pltpu
from jax.sharding import PartitionSpec as P

REACH = 2
WINDOW = 2 * REACH + 1
EPS = 1e-06
ROWS = 128
COLS = 128
GROUP = 8
SIDE = 8
CELLS = SIDE * SIDE
COUNT = GROUP * CELLS
BATCH = ROWS * COUNT
WIDTH = GROUP * COLS
TILE = 16
HALF = ROWS // 2
FAR_FIRST = (4, 5, 3, 2, 6, 7, 1)
SIDE_FAR_FIRST = (4, 3, 5, 2, 6, 1, 7)
PLANE = [(down, over) for down in SIDE_FAR_FIRST + (0,) for over in SIDE_FAR_FIRST + (0,) if down or over]

F32 = jnp.float32
BF16 = jnp.bfloat16


def remote(src, dst, send_sem, recv_sem, device):
    return pltpu.make_async_remote_copy(
        src_ref=src,
        dst_ref=dst,
        send_sem=send_sem,
        recv_sem=recv_sem,
        device_id=(device,),
        device_id_type=pl.DeviceIdType.MESH,
    )


def dot(left, right, dims):
    return lax.dot_general(left, right, (dims, ((), ())), preferred_element_type=F32)


def softplus_parts(logits):
    tail = jnp.exp(-jnp.abs(logits))
    share = 1.0 / (1.0 + tail)
    sigmoid = jnp.where(logits >= 0, share, tail * share)
    return jnp.log1p(tail), sigmoid


def kernel(
    feat_hbm, head_hbm, pose_hbm, ids_hbm, scale_ref, bias_ref,
    pose_grad_hbm, head_grad_ref, loss_ref, scale_grad_ref,
    feats, feats_t, pose_raw, poses, embs, pose_held, emb_held, pose_out, ids, head_rows, piece_src, piece, tile_f32, head,
    proj_src, proj, unit, inv_pose, gp_src, gp, part_src, part, fin_src, fin,
    tot_src, tot_group, tot_z_src, tot_z, tot_y_src, tot_y,
    local_sem, piece_s, piece_r, feat_s, feat_r, head_s, head_r, pose_s, pose_r, emb_s, emb_r,
    proj_s, proj_r, gp_s, gp_r, part_s, part_r, fin_s, fin_r, tot_s, tot_r,
):
    me = lax.axis_index("dp")
    slot = lax.rem(me, GROUP)
    cell = me // GROUP
    y = cell // SIDE
    z = lax.rem(cell, SIDE)
    core = lax.rem(me, 2)
    base = me - slot
    sibling = me + 1 - 2 * core
    lines = [lax.rem(y + step, SIDE) * SIDE for step in range(SIDE)]
    spots = [lax.rem(z + step, SIDE) for step in range(SIDE)]

    def mate_slot(step):
        return lax.rem(slot + step, GROUP)

    def turned(place, step):
        return lax.rem(place + step, SIDE)

    def at(of_y, of_z):
        return (of_y * SIDE + of_z) * GROUP + slot

    def ring(step):
        return lax.rem(me + step + COUNT, COUNT)

    loads = [
        pltpu.make_async_copy(source, target, local_sem.at[number])
        for number, (source, target) in enumerate((
            (head_hbm, head_rows),
            (feat_hbm, feats.at[slot]),
            (pose_hbm, pose_raw),
            (ids_hbm, ids),
        ))
    ]
    load_head, load_feat, load_pose, load_ids = loads
    for load in loads:
        load.start()

    barrier = pltpu.get_barrier_semaphore()

    def greet(device):
        pl.semaphore_signal(barrier, inc=1, device_id=(device,), device_id_type=pl.DeviceIdType.MESH)

    for step in FAR_FIRST:
        greet(base + mate_slot(step))
    for down, over in PLANE:
        greet((lines[down] + spots[over]) * GROUP + slot)

    load_head.wait()
    rows = head_rows[...].astype(F32)
    piece_src[...] = jnp.zeros_like(piece_src)
    for number in range(GROUP):
        piece_src[number, 0:2, :] = rows[:, number * COLS : (number + 1) * COLS]
    piece[slot] = piece_src[slot]

    pl.semaphore_wait(barrier, GROUP - 1 + CELLS - 1)

    def exchange(blocks, held, sems, semr):
        own = blocks.at[REACH]
        ahead = remote(own, blocks.at[0], sems.at[0], semr.at[0], ring(2))
        behind = remote(own, blocks.at[4], sems.at[1], semr.at[4], ring(-2))
        ahead_cell = remote(own, held, sems.at[0], semr.at[2], ring(GROUP))
        behind_cell = remote(own, held, sems.at[1], semr.at[2], ring(-GROUP))
        ahead_relay = remote(held, blocks.at[0], sems.at[4], semr.at[0], base + core)
        behind_relay = remote(held, blocks.at[4], sems.at[4], semr.at[4], base + GROUP - 2 + core)
        beside = remote(own, blocks.at[1 + 2 * core], sems.at[2], semr.at[1 + 2 * core], sibling)
        passed = remote(
            blocks.at[4 - 4 * core], blocks.at[3 - 2 * core], sems.at[3], semr.at[3 - 2 * core], sibling
        )

        def to_cells():
            pl.when(slot >= GROUP - 2)(ahead_cell.start)
            pl.when(slot < 2)(behind_cell.start)

        def direct():
            pl.when(slot < GROUP - 2)(ahead.start)
            pl.when(slot >= 2)(behind.start)
            beside.start()

        def relay():
            @pl.when(slot >= GROUP - 2)
            def _():
                ahead_cell.wait_recv()
                ahead_relay.start()

            @pl.when(slot < 2)
            def _():
                behind_cell.wait_recv()
                behind_relay.start()

        def forward():
            ahead.wait_recv()
            behind.wait_recv()
            passed.start()

        def finish():
            remote(own, blocks.at[1], sems.at[2], semr.at[1], sibling).wait_recv()
            remote(own, blocks.at[3], sems.at[3], semr.at[3], sibling).wait_recv()

        def drain():
            ahead.wait_send()
            behind.wait_send()
            beside.wait_send()
            passed.wait_send()
            pl.when(slot >= GROUP - 2)(ahead_relay.wait_send)
            pl.when(slot < 2)(behind_relay.wait_send)

        return to_cells, direct, relay, forward, finish, drain

    pose_to_cells, pose_direct, pose_relay, pose_forward, pose_finish, pose_drain = exchange(
        poses, pose_held, pose_s, pose_r
    )
    emb_to_cells, emb_direct, emb_relay, emb_forward, emb_finish, emb_drain = exchange(embs, emb_held, emb_s, emb_r)

    piece_copies = []
    for step in FAR_FIRST:
        to = mate_slot(step)
        copy = remote(piece_src.at[to], piece.at[slot], piece_s.at[step], piece_r.at[step], base + to)
        copy.start()
        piece_copies.append(copy)

    load_feat.wait()
    right = base + mate_slot(2)
    left = base + mate_slot(6)

    def half(of_slot, number):
        return feats.at[of_slot, pl.ds(number * HALF, HALF), :]

    def send_half(of_slot, number, device, sem):
        copy = remote(half(of_slot, number), half(of_slot, number), feat_s.at[sem], feat_r.at[sem], device)
        copy.start()
        return copy

    def send_block(of_slot, sem):
        copy = remote(feats.at[of_slot], feats.at[of_slot], feat_s.at[sem], feat_r.at[sem], sibling)
        copy.start()
        return copy

    right_a = send_half(slot, 0, right, 0)
    left_b = send_half(slot, 1, left, 1)
    right_b = send_half(slot, 1, right, 2)
    left_a = send_half(slot, 0, left, 3)
    block_own = send_block(slot, 6)

    load_pose.wait()
    raw = pose_raw[...].astype(F32)
    inv_p = 1.0 / jnp.sqrt(jnp.sum(raw * raw, axis=1, keepdims=True) + EPS)
    inv_pose[...] = jnp.broadcast_to(inv_p, (ROWS, COLS))
    poses[REACH] = (raw * inv_p).astype(BF16)
    pose_to_cells()

    for copy in piece_copies:
        copy.wait_recv()
    for number in range(GROUP):
        tile_f32[2 * number : 2 * number + 2, :] = piece[number, 0:2, :]
    head[cell] = tile_f32[...].astype(BF16)
    for down, over in PLANE:
        device = (lines[down] + spots[over]) * GROUP + slot
        remote(head.at[cell], head.at[cell], head_s, head_r, device).start()

    right_a.wait_recv()
    right_a2 = send_half(mate_slot(6), 0, right, 4)
    left_b.wait_recv()
    left_b2 = send_half(mate_slot(2), 1, left, 5)

    pose_direct()
    pose_relay()

    right_b.wait_recv()
    block_left = send_block(mate_slot(6), 7)
    left_a.wait_recv()
    block_right = send_block(mate_slot(2), 8)
    right_a2.wait_recv()
    left_b2.wait_recv()
    block_far = send_block(mate_slot(4), 9)

    pltpu.make_async_copy(head.at[pl.ds(0, CELLS - 1)], head.at[pl.ds(0, CELLS - 1)], head_r).wait()
    for copy in (block_own, block_left, block_right, block_far):
        copy.wait_recv()
    proj_copies = []
    for step in FAR_FIRST:
        to = mate_slot(step)
        proj_src[step] = dot(feats[to], head[...].reshape(WIDTH, COLS), ((1,), (0,)))
        copy = remote(proj_src.at[step], proj.at[slot], proj_s.at[step], proj_r.at[step], base + to)
        copy.start()
        proj_copies.append(copy)
    proj[slot] = dot(feats[slot], head[...].reshape(WIDTH, COLS), ((1,), (0,)))

    pose_forward()
    for number in range(GROUP):
        feats_t[:, number * ROWS : (number + 1) * ROWS] = feats[number].T
    load_ids.wait()
    pose_finish()
    for copy in proj_copies:
        copy.wait_recv()

    square = jnp.zeros((ROWS, COLS), F32)
    for number in range(GROUP):
        value = proj[number]
        square = square + value * value
    inv_i = 1.0 / jnp.sqrt(jnp.sum(square, axis=1, keepdims=True) + EPS)
    for number in range(GROUP):
        value = proj[number] * inv_i
        unit[:, number * COLS : (number + 1) * COLS] = value
        embs[REACH, :, number * COLS : (number + 1) * COLS] = value.astype(BF16)
    emb_to_cells()

    scale = jnp.broadcast_to(scale_ref[...], (ROWS, ROWS))
    bias = jnp.broadcast_to(bias_ref[...], (ROWS, ROWS))

    def ids_of(step):
        return ids[pl.ds(ring(step), 1), :]

    own_ids = jnp.broadcast_to(ids_of(0), (ROWS, ROWS)).T

    def window_terms(left_emb, blocks, with_totals):
        weights = []
        totals = [jnp.zeros((1, COLS), F32) for _ in range(3)]
        for number in range(WINDOW):
            inner = dot(left_emb, blocks[number], ((1,), (1,)))
            logits = scale * inner + bias
            matched = own_ids == ids_of(number - REACH)
            tail, sigmoid = softplus_parts(logits)
            gradient = sigmoid - matched.astype(F32)
            weights.append((scale * gradient).astype(BF16))
            if with_totals:
                signed = jnp.where(matched, logits, -logits)
                loss = tail - jnp.minimum(signed, 0.0)
                for place, term in enumerate((loss, gradient, gradient * inner)):
                    totals[place] = totals[place] + jnp.sum(term, axis=0, keepdims=True)
        return jnp.concatenate(weights, axis=1), totals

    weight, totals = window_terms(embs[REACH], poses, True)
    grad_img = dot(weight, poses[...].reshape(WINDOW * ROWS, WIDTH), ((1,), (0,)))
    unit_img = unit[...]
    along = jnp.sum(unit_img * grad_img, axis=1, keepdims=True)
    grad_proj = ((grad_img - unit_img * along) * inv_i).astype(BF16)
    for number in range(GROUP):
        gp_src[number] = grad_proj[:, number * COLS : (number + 1) * COLS]
    gp_copies = []
    for step in FAR_FIRST:
        to = mate_slot(step)
        copy = remote(gp_src.at[to], gp.at[slot], gp_s.at[step], gp_r.at[step], base + to)
        copy.start()
        gp_copies.append(copy)
    gp[slot] = gp_src[slot]

    tot_src[...] = jnp.zeros_like(tot_src)
    for place in range(3):
        tot_src[place : place + 1, :] = totals[place]
    tot_copies = []
    for step in FAR_FIRST:
        copy = remote(tot_src, tot_group.at[slot], tot_s.at[step], tot_r.at[step], base + mate_slot(step))
        copy.start()
        tot_copies.append(copy)
    tot_group[slot] = tot_src[...]

    for copy in gp_copies:
        copy.wait_recv()
    emb_direct()
    for of_y in range(SIDE):
        value = dot(feats_t[of_y * ROWS : (of_y + 1) * ROWS, :], gp[...].reshape(GROUP * ROWS, COLS), ((1,), (0,)))
        part_src[of_y * SIDE : (of_y + 1) * SIDE] = value.astype(BF16).reshape(SIDE, TILE, COLS)
    for down, over in PLANE:
        to = lines[down] + spots[over]
        remote(part_src.at[to], part.at[cell], part_s, part_r, to * GROUP + slot).start()
    part[cell] = part_src[cell]
    emb_relay()

    for copy in tot_copies:
        copy.wait_recv()
    group_sum = tot_group[0]
    for number in range(1, GROUP):
        group_sum = group_sum + tot_group[number]
    tot_z_src[...] = group_sum
    tot_z[z] = group_sum
    z_copies = []
    for step in SIDE_FAR_FIRST:
        copy = remote(tot_z_src, tot_z.at[z], tot_s.at[8 + step], tot_r.at[8 + step], at(y, turned(z, step)))
        copy.start()
        z_copies.append(copy)

    emb_forward()
    for copy in z_copies:
        copy.wait_recv()
    z_sum = tot_z[0]
    for number in range(1, SIDE):
        z_sum = z_sum + tot_z[number]
    tot_y_src[...] = z_sum
    tot_y[y] = z_sum
    y_copies = []
    for step in SIDE_FAR_FIRST:
        copy = remote(tot_y_src, tot_y.at[y], tot_s.at[16 + step], tot_r.at[16 + step], at(turned(y, step), z))
        copy.start()
        y_copies.append(copy)

    pltpu.make_async_copy(part.at[pl.ds(0, CELLS - 1)], part.at[pl.ds(0, CELLS - 1)], part_r).wait()

    summed = jnp.sum(part[...].astype(F32), axis=0)
    fin_src[...] = jnp.zeros_like(fin_src)
    for number in range(GROUP):
        fin_src[number, 0:2, :] = summed[2 * number : 2 * number + 2, :]
    fin_copies = []
    for step in FAR_FIRST:
        to = mate_slot(step)
        copy = remote(fin_src.at[to], fin.at[slot], fin_s.at[step], fin_r.at[step], base + to)
        copy.start()
        fin_copies.append(copy)
    fin[slot] = fin_src[slot]

    emb_finish()
    pose_weight, _ = window_terms(poses[REACH], embs, False)
    grad_pose = dot(pose_weight, embs[...].reshape(WINDOW * ROWS, WIDTH), ((1,), (0,)))
    inv_q = inv_pose[:, 0:1]
    unit_pose = pose_raw[...].astype(F32) * inv_q
    along_pose = jnp.sum(unit_pose * grad_pose, axis=1, keepdims=True)
    pose_out[...] = ((grad_pose - unit_pose * along_pose) * inv_q).astype(BF16)
    store_pose = pltpu.make_async_copy(pose_out, pose_grad_hbm, local_sem.at[4])
    store_pose.start()

    for copy in y_copies:
        copy.wait_recv()
    y_sum = tot_y[0]
    for number in range(1, SIDE):
        y_sum = y_sum + tot_y[number]
    y_sum = y_sum / BATCH
    loss_ref[0] = jnp.sum(y_sum[0:1, :])
    loss_ref[1] = jnp.sum(y_sum[1:2, :])
    scale_grad_ref[0] = jnp.sum(y_sum[2:3, :])

    for copy in fin_copies:
        copy.wait_recv()
    for number in range(GROUP):
        head_grad_ref[:, number * COLS : (number + 1) * COLS] = fin[number, 0:2, :]

    store_pose.wait()
    for copy in piece_copies + proj_copies + gp_copies + fin_copies:
        copy.wait_send()
    for copy in tot_copies + z_copies + y_copies:
        copy.wait_send()
    for copy in (right_a, left_b, right_b, left_a, right_a2, left_b2, block_own, block_left, block_right, block_far):
        copy.wait_send()
    pose_drain()
    emb_drain()
    pltpu.make_async_copy(head.at[pl.ds(0, CELLS - 1)], head.at[pl.ds(0, CELLS - 1)], head_s).wait()
    pltpu.make_async_copy(part_src.at[pl.ds(0, CELLS - 1)], part_src.at[pl.ds(0, CELLS - 1)], part_s).wait()


def local(features, head_rows, poses, match_ids, logit_scale, logit_bias):
    vmem = pl.BlockSpec(memory_space=pltpu.VMEM)
    smem = pl.BlockSpec(memory_space=pltpu.SMEM)
    hbm = pl.BlockSpec(memory_space=pltpu.HBM)
    dma = pltpu.SemaphoreType.DMA
    block = (ROWS, WIDTH)
    square = (GROUP, ROWS, COLS)
    shapes = (
        jax.ShapeDtypeStruct(block, BF16),
        jax.ShapeDtypeStruct((2, WIDTH), F32),
        jax.ShapeDtypeStruct((2,), F32),
        jax.ShapeDtypeStruct((1,), F32),
    )
    return pl.pallas_call(
        kernel,
        name="contrastive",
        out_shape=shapes,
        in_specs=[hbm, hbm, hbm, hbm, vmem, vmem],
        out_specs=(hbm, vmem, smem, smem),
        scratch_shapes=[
            pltpu.VMEM((GROUP,) + block, BF16),
            pltpu.VMEM((WIDTH, GROUP * ROWS), BF16),
            pltpu.VMEM(block, BF16),
            pltpu.VMEM((WINDOW,) + block, BF16),
            pltpu.VMEM((WINDOW,) + block, BF16),
            pltpu.VMEM(block, BF16),
            pltpu.VMEM(block, BF16),
            pltpu.VMEM(block, BF16),
            pltpu.VMEM((COUNT, ROWS), jnp.int32),
            pltpu.VMEM((2, WIDTH), BF16),
            pltpu.VMEM((GROUP, 8, COLS), F32),
            pltpu.VMEM((GROUP, 8, COLS), F32),
            pltpu.VMEM((TILE, COLS), F32),
            pltpu.VMEM((CELLS, TILE, COLS), BF16),
            pltpu.VMEM(square, F32),
            pltpu.VMEM(square, F32),
            pltpu.VMEM(block, F32),
            pltpu.VMEM((ROWS, COLS), F32),
            pltpu.VMEM(square, BF16),
            pltpu.VMEM(square, BF16),
            pltpu.VMEM((CELLS, TILE, COLS), BF16),
            pltpu.VMEM((CELLS, TILE, COLS), BF16),
            pltpu.VMEM((GROUP, 8, COLS), F32),
            pltpu.VMEM((GROUP, 8, COLS), F32),
            pltpu.VMEM((8, COLS), F32),
            pltpu.VMEM((GROUP, 8, COLS), F32),
            pltpu.VMEM((8, COLS), F32),
            pltpu.VMEM((SIDE, 8, COLS), F32),
            pltpu.VMEM((8, COLS), F32),
            pltpu.VMEM((SIDE, 8, COLS), F32),
            dma((5,)),
            dma((GROUP,)), dma((GROUP,)),
            dma((10,)), dma((10,)),
            dma, dma,
            dma((WINDOW,)), dma((WINDOW,)),
            dma((WINDOW,)), dma((WINDOW,)),
            dma((GROUP,)), dma((GROUP,)),
            dma((GROUP,)), dma((GROUP,)),
            dma, dma,
            dma((GROUP,)), dma((GROUP,)),
            dma((24,)), dma((24,)),
        ],
        compiler_params=pltpu.CompilerParams(
            collective_id=0, has_side_effects=True, vmem_limit_bytes=53 * 1024 * 1024 + 512 * 1024
        ),
    )(features, head_rows, poses, match_ids.reshape(COUNT, ROWS), logit_scale.reshape(1, 1), logit_bias.reshape(1, 1))


def solution(mesh):
    return jax.shard_map(
        local,
        mesh=mesh,
        in_specs=(P("dp", None), P("dp", None), P("dp", None), P(), P(), P()),
        out_specs=(P("dp", None), P("dp", None), P(), P()),
        check_vma=False,
    )
```

time: 80.6 us -> 71 us (0.88); the launches traced: 80.3 us -> 69.8 us
  Pallas kernels: 72 us -> 64.2 us
  local copies, waits for them, and re-layouts: 4.66 us -> 1.84 us
    pallas_call x1, Pallas kernels: 72 us -> 64.2 us  [local(): pl.pallas_call(kernel, name='contrastive', out_shape=shapes, in_specs=[hb...]
    unnamed x11 -> x5, local copies, waits for them, and re-layouts: 4.66 us -> 1.84 us
where the time goes in v2:
time: 71 us; the launch traced here: 69.8 us
  Pallas kernels  64.2 us (90%)
  between operations  3.72 us (5%)
  local copies, waits for them, and re-layouts  1.84 us (3%)
    pallas_call x1, Pallas kernels, local(): pl.pallas_call(kernel, name='contrastive', out_shape=shapes, in_specs=[hb...  64.2 us
    unnamed x5, local copies, waits for them, and re-layouts  1.84 us

profile of v2, /device:TPU:1, one launch (start us, length us, event | category | flops | bytes accessed | tf_op | source)
XLA Modules:
  0.0 69.8 jit_solution(803232415610908158)
XLA Ops:
  1.3 0.0 copy-start
  1.9 0.0 copy-done
  2.0 64.2 %contrastive.1 = (bf16[128,1024]{1,0:T(8,128)(2,1)S(1)}, f32[2,1024]{1,0:T(2,128)S(1)}, f32[2]{0:T(128)S(1)}, f32[1]{0:T(128)}) custom-call(bf16[128,1024]{1,0:T(8,128)(2,1)} %feat_hbm.1, bf16[2,1024]{1,0:T(2,128)(2,1)S(1)} %copy-done, bf16[128,1024]{1,0:T(8,128)(2,1)} %pose_hbm.1, s32[512,128]{1,0:T(8,128)} %bitcast.5, f32[1,1]{1,0:T(1,128)} %bitcast.3.scale_ref, ...), custom_call_target="tpu_custom_call" | custom-call | tf_op jit(solution)/shard_map/contrastive/pallas_call | solution.py:419
  66.2 0.7 %copy.16 = bf16[128,1024]{1,0:T(8,128)(2,1)} copy(bf16[128,1024]{1,0:T(8,128)(2,1)S(1)} %get-tuple-element.8) | data formatting | bytes 524288
  66.9 0.6 copy.17
  67.5 0.5 copy.18
Async XLA Ops:
  1.3 0.7 copy-start

commit v3 on v2

--- a/solution.py
+++ b/solution.py
@@ -18,6 +18,8 @@
 WIDTH = GROUP * COLS
 TILE = 16
 HALF = ROWS // 2
+LEVELS = 32767.0
+SMALLEST = 1e-33
 FAR_FIRST = (4, 5, 3, 2, 6, 7, 1)
 SIDE_FAR_FIRST = (4, 3, 5, 2, 6, 1, 7)
 PLANE = [(down, over) for down in SIDE_FAR_FIRST + (0,) for over in SIDE_FAR_FIRST + (0,) if down or over]
@@ -52,7 +54,7 @@
     feat_hbm, head_hbm, pose_hbm, ids_hbm, scale_ref, bias_ref,
     pose_grad_hbm, head_grad_ref, loss_ref, scale_grad_ref,
     feats, feats_t, pose_raw, poses, embs, pose_held, emb_held, pose_out, ids, head_rows, piece_src, piece, tile_f32, head,
-    proj_src, proj, unit, inv_pose, gp_src, gp, part_src, part, fin_src, fin,
+    proj_src, proj, peak_src, peaks, peak_rows, unit, inv_pose, gp_src, gp, part_src, part, fin_src, fin,
     tot_src, tot_group, tot_z_src, tot_z, tot_y_src, tot_y,
     local_sem, piece_s, piece_r, feat_s, feat_r, head_s, head_r, pose_s, pose_r, emb_s, emb_r,
     proj_s, proj_r, gp_s, gp_r, part_s, part_r, fin_s, fin_r, tot_s, tot_r,
@@ -103,6 +105,7 @@
     for down, over in PLANE:
         greet((lines[down] + spots[over]) * GROUP + slot)
 
+    peak_rows[...] = jnp.zeros_like(peak_rows)
     load_head.wait()
     rows = head_rows[...].astype(F32)
     piece_src[...] = jnp.zeros_like(piece_src)
@@ -113,54 +116,77 @@
     pl.semaphore_wait(barrier, GROUP - 1 + CELLS - 1)
 
     def exchange(blocks, held, sems, semr):
-        own = blocks.at[REACH]
-        ahead = remote(own, blocks.at[0], sems.at[0], semr.at[0], ring(2))
-        behind = remote(own, blocks.at[4], sems.at[1], semr.at[4], ring(-2))
-        ahead_cell = remote(own, held, sems.at[0], semr.at[2], ring(GROUP))
-        behind_cell = remote(own, held, sems.at[1], semr.at[2], ring(-GROUP))
-        ahead_relay = remote(held, blocks.at[0], sems.at[4], semr.at[0], base + core)
-        behind_relay = remote(held, blocks.at[4], sems.at[4], semr.at[4], base + GROUP - 2 + core)
-        beside = remote(own, blocks.at[1 + 2 * core], sems.at[2], semr.at[1 + 2 * core], sibling)
-        passed = remote(
-            blocks.at[4 - 4 * core], blocks.at[3 - 2 * core], sems.at[3], semr.at[3 - 2 * core], sibling
+        def part_of(place, number):
+            return blocks.at[place, pl.ds(number * HALF, HALF), :]
+
+        def pair(make):
+            return [make(number) for number in range(2)]
+
+        def held_part(number):
+            return held.at[pl.ds(number * HALF, HALF), :]
+
+        last = GROUP - 2
+        ahead = pair(lambda n: remote(part_of(REACH, n), part_of(0, n), sems.at[n], semr.at[n], ring(2)))
+        behind = pair(lambda n: remote(part_of(REACH, n), part_of(4, n), sems.at[2 + n], semr.at[8 + n], ring(-2)))
+        ahead_cell = pair(lambda n: remote(part_of(REACH, n), held_part(n), sems.at[n], semr.at[4 + n], ring(GROUP)))
+        behind_cell = pair(
+            lambda n: remote(part_of(REACH, n), held_part(n), sems.at[2 + n], semr.at[4 + n], ring(-GROUP))
         )
+        ahead_relay = pair(lambda n: remote(held_part(n), part_of(0, n), sems.at[8 + n], semr.at[n], base + core))
+        behind_relay = pair(
+            lambda n: remote(held_part(n), part_of(4, n), sems.at[8 + n], semr.at[8 + n], base + last + core)
+        )
+        to_own = 1 + 2 * core
+        to_pass = 3 - 2 * core
+        beside = pair(
+            lambda n: remote(part_of(REACH, n), part_of(to_own, n), sems.at[4 + n], semr.at[2 * to_own + n], sibling)
+        )
+        far = 4 - 4 * core
+        passed = pair(
+            lambda n: remote(part_of(far, n), part_of(to_pass, n), sems.at[6 + n], semr.at[2 * to_pass + n], sibling)
+        )
+
+        def arrived(place, number):
+            remote(part_of(REACH, number), part_of(place, number), sems.at[0], semr.at[2 * place + number], sibling).wait_recv()
 
         def to_cells():
-            pl.when(slot >= GROUP - 2)(ahead_cell.start)
-            pl.when(slot < 2)(behind_cell.start)
+            for number in range(2):
+                pl.when(slot >= last)(ahead_cell[number].start)
+                pl.when(slot < 2)(behind_cell[number].start)
 
         def direct():
-            pl.when(slot < GROUP - 2)(ahead.start)
-            pl.when(slot >= 2)(behind.start)
-            beside.start()
-
-        def relay():
-            @pl.when(slot >= GROUP - 2)
+            for number in range(2):
+                pl.when(slot < last)(ahead[number].start)
+                pl.when(slot >= 2)(behind[number].start)
+            for number in range(2):
+                beside[number].start()
+
+        def relay(number):
+            @pl.when(slot >= last)
             def _():
-                ahead_cell.wait_recv()
-                ahead_relay.start()
+                ahead_cell[number].wait_recv()
+                ahead_relay[number].start()
 
             @pl.when(slot < 2)
             def _():
-                behind_cell.wait_recv()
-                behind_relay.start()
-
-        def forward():
-            ahead.wait_recv()
-            behind.wait_recv()
-            passed.start()
+                behind_cell[number].wait_recv()
+                behind_relay[number].start()
+
+        def forward(number):
+            arrived(far, number)
+            passed[number].start()
 
         def finish():
-            remote(own, blocks.at[1], sems.at[2], semr.at[1], sibling).wait_recv()
-            remote(own, blocks.at[3], sems.at[3], semr.at[3], sibling).wait_recv()
+            for number in range(2):
+                for place in (4 * core, 1, 3):
+                    arrived(place, number)
 
         def drain():
-            ahead.wait_send()
-            behind.wait_send()
-            beside.wait_send()
-            passed.wait_send()
-            pl.when(slot >= GROUP - 2)(ahead_relay.wait_send)
-            pl.when(slot < 2)(behind_relay.wait_send)
+            for number in range(2):
+                for copies in (ahead, behind, beside, passed):
+                    copies[number].wait_send()
+                pl.when(slot >= last)(ahead_relay[number].wait_send)
+                pl.when(slot < 2)(behind_relay[number].wait_send)
 
         return to_cells, direct, relay, forward, finish, drain
 
@@ -221,7 +247,8 @@
     left_b2 = send_half(mate_slot(2), 1, left, 5)
 
     pose_direct()
-    pose_relay()
+    pose_relay(0)
+    pose_relay(1)
 
     right_b.wait_recv()
     block_left = send_block(mate_slot(6), 7)
@@ -234,16 +261,33 @@
     pltpu.make_async_copy(head.at[pl.ds(0, CELLS - 1)], head.at[pl.ds(0, CELLS - 1)], head_r).wait()
     for copy in (block_own, block_left, block_right, block_far):
         copy.wait_recv()
+    lane = lax.broadcasted_iota(jnp.int32, (ROWS, COLS), 1)
+    peak_columns = jnp.zeros((ROWS, COLS), F32)
     proj_copies = []
+    for step in FAR_FIRST + (0,):
+        to = mate_slot(step)
+        value = dot(feats[to], head[...].reshape(WIDTH, COLS), ((1,), (0,)))
+        peak = jnp.maximum(jnp.max(jnp.abs(value), axis=1, keepdims=True), SMALLEST)
+        coded = jnp.round(value * (LEVELS / peak)).astype(jnp.int32).astype(jnp.int16)
+        peak_columns = jnp.where(lane == to, peak, peak_columns)
+        if step:
+            proj_src[step] = coded
+            copy = remote(proj_src.at[step], proj.at[slot], proj_s.at[step], proj_r.at[step], base + to)
+            copy.start()
+            proj_copies.append(copy)
+        else:
+            proj[slot] = coded
+    peak_src[...] = peak_columns.T[0:GROUP, :]
+    peaks[slot] = peak_src[...]
     for step in FAR_FIRST:
-        to = mate_slot(step)
-        proj_src[step] = dot(feats[to], head[...].reshape(WIDTH, COLS), ((1,), (0,)))
-        copy = remote(proj_src.at[step], proj.at[slot], proj_s.at[step], proj_r.at[step], base + to)
+        copy = remote(
+            peak_src, peaks.at[slot], proj_s.at[GROUP + step], proj_r.at[GROUP + step], base + mate_slot(step)
+        )
         copy.start()
         proj_copies.append(copy)
-    proj[slot] = dot(feats[slot], head[...].reshape(WIDTH, COLS), ((1,), (0,)))
-
-    pose_forward()
+
+    pose_forward(0)
+    pose_forward(1)
     for number in range(GROUP):
         feats_t[:, number * ROWS : (number + 1) * ROWS] = feats[number].T
     load_ids.wait()
@@ -251,15 +295,20 @@
     for copy in proj_copies:
         copy.wait_recv()
 
+    for number in range(GROUP):
+        peak_rows[number : number + 1, :] = peaks[number, pl.ds(slot, 1), :]
+    unscale = peak_rows[...].T / LEVELS
     square = jnp.zeros((ROWS, COLS), F32)
     for number in range(GROUP):
-        value = proj[number]
+        value = proj[number].astype(jnp.int32).astype(F32) * unscale[:, number : number + 1]
+        unit[:, number * COLS : (number + 1) * COLS] = value
         square = square + value * value
     inv_i = 1.0 / jnp.sqrt(jnp.sum(square, axis=1, keepdims=True) + EPS)
     for number in range(GROUP):
-        value = proj[number] * inv_i
-        unit[:, number * COLS : (number + 1) * COLS] = value
-        embs[REACH, :, number * COLS : (number + 1) * COLS] = value.astype(BF16)
+        columns = slice(number * COLS, (number + 1) * COLS)
+        value = unit[:, columns] * inv_i
+        unit[:, columns] = value
+        embs[REACH, :, columns] = value.astype(BF16)
     emb_to_cells()
 
     scale = jnp.broadcast_to(scale_ref[...], (ROWS, ROWS))
@@ -315,6 +364,7 @@
     for copy in gp_copies:
         copy.wait_recv()
     emb_direct()
+    emb_relay(0)
     for of_y in range(SIDE):
         value = dot(feats_t[of_y * ROWS : (of_y + 1) * ROWS, :], gp[...].reshape(GROUP * ROWS, COLS), ((1,), (0,)))
         part_src[of_y * SIDE : (of_y + 1) * SIDE] = value.astype(BF16).reshape(SIDE, TILE, COLS)
@@ -322,7 +372,7 @@
         to = lines[down] + spots[over]
         remote(part_src.at[to], part.at[cell], part_s, part_r, to * GROUP + slot).start()
     part[cell] = part_src[cell]
-    emb_relay()
+    emb_relay(1)
 
     for copy in tot_copies:
         copy.wait_recv()
@@ -337,7 +387,8 @@
         copy.start()
         z_copies.append(copy)
 
-    emb_forward()
+    emb_forward(0)
+    emb_forward(1)
     for copy in z_copies:
         copy.wait_recv()
     z_sum = tot_z[0]
@@ -437,8 +488,11 @@
             pltpu.VMEM((GROUP, 8, COLS), F32),
             pltpu.VMEM((TILE, COLS), F32),
             pltpu.VMEM((CELLS, TILE, COLS), BF16),
-            pltpu.VMEM(square, F32),
-            pltpu.VMEM(square, F32),
+            pltpu.VMEM(square, jnp.int16),
+            pltpu.VMEM(square, jnp.int16),
+            pltpu.VMEM((GROUP, COLS), F32),
+            pltpu.VMEM((GROUP, GROUP, COLS), F32),
+            pltpu.VMEM((ROWS, COLS), F32),
             pltpu.VMEM(block, F32),
             pltpu.VMEM((ROWS, COLS), F32),
             pltpu.VMEM(square, BF16),
@@ -457,9 +511,9 @@
             dma((GROUP,)), dma((GROUP,)),
             dma((10,)), dma((10,)),
             dma, dma,
-            dma((WINDOW,)), dma((WINDOW,)),
-            dma((WINDOW,)), dma((WINDOW,)),
-            dma((GROUP,)), dma((GROUP,)),
+            dma((2 * WINDOW,)), dma((2 * WINDOW,)),
+            dma((2 * WINDOW,)), dma((2 * WINDOW,)),
+            dma((2 * GROUP,)), dma((2 * GROUP,)),
             dma((GROUP,)), dma((GROUP,)),
             dma, dma,
             dma((GROUP,)), dma((GROUP,)),

time: 71 us -> 67.7 us (0.954); the launches traced: 69.8 us -> 67.6 us
  Pallas kernels: 64.2 us -> 62 us
    pallas_call x1, Pallas kernels: 64.2 us -> 62 us  [local(): pl.pallas_call(kernel, name='contrastive', out_shape=shapes, in_specs=[hb...]
where the time goes in v3:
time: 67.7 us; the launch traced here: 67.6 us
  Pallas kernels  62 us (92%)
  between operations  3.72 us (5%)
  local copies, waits for them, and re-layouts  1.84 us (3%)
    pallas_call x1, Pallas kernels, local(): pl.pallas_call(kernel, name='contrastive', out_shape=shapes, in_specs=[hb...  62 us
    unnamed x5, local copies, waits for them, and re-layouts  1.84 us

profile of v3, /device:TPU:1, one launch (start us, length us, event | category | flops | bytes accessed | tf_op | source)
XLA Modules:
  0.0 67.6 jit_solution(4279038614241298771)
XLA Ops:
  1.3 0.0 copy-start
  1.9 0.0 copy-done
  2.0 62.0 %contrastive.1 = (bf16[128,1024]{1,0:T(8,128)(2,1)S(1)}, f32[2,1024]{1,0:T(2,128)S(1)}, f32[2]{0:T(128)S(1)}, f32[1]{0:T(128)}) custom-call(bf16[128,1024]{1,0:T(8,128)(2,1)} %feat_hbm.1, bf16[2,1024]{1,0:T(2,128)(2,1)S(1)} %copy-done, bf16[128,1024]{1,0:T(8,128)(2,1)} %pose_hbm.1, s32[512,128]{1,0:T(8,128)} %bitcast.5, f32[1,1]{1,0:T(1,128)} %bitcast.3.scale_ref, ...), custom_call_target="tpu_custom_call" | custom-call | tf_op jit(solution)/shard_map/contrastive/pallas_call | solution.py:470
  64.0 0.7 %copy.16 = bf16[128,1024]{1,0:T(8,128)(2,1)} copy(bf16[128,1024]{1,0:T(8,128)(2,1)S(1)} %get-tuple-element.8) | data formatting | bytes 524288
  64.7 0.6 copy.17
  65.3 0.5 copy.18
Async XLA Ops:
  1.3 0.7 %copy-start = (bf16[2,1024]{1,0:T(2,128)(2,1)S(1)}, bf16[2,1024]{1,0:T(2,128)(2,1)}, u32[]{:S(2)}) copy-start(bf16[2,1024]{1,0:T(2,128)(2,1)} %head_hbm.1) | copy-start | bytes 12292

commit v4 on v3

--- a/solution.py
+++ b/solution.py
@@ -291,6 +291,15 @@
     for number in range(GROUP):
         feats_t[:, number * ROWS : (number + 1) * ROWS] = feats[number].T
     load_ids.wait()
+    scale = jnp.broadcast_to(scale_ref[...], (ROWS, ROWS))
+    bias = jnp.broadcast_to(bias_ref[...], (ROWS, ROWS))
+
+    def ids_of(step):
+        return ids[pl.ds(ring(step), 1), :]
+
+    own_ids = jnp.broadcast_to(ids_of(0), (ROWS, ROWS)).T
+    tot_src[...] = jnp.zeros_like(tot_src)
+    fin_src[...] = jnp.zeros_like(fin_src)
     pose_finish()
     for copy in proj_copies:
         copy.wait_recv()
@@ -311,32 +320,30 @@
         embs[REACH, :, columns] = value.astype(BF16)
     emb_to_cells()
 
-    scale = jnp.broadcast_to(scale_ref[...], (ROWS, ROWS))
-    bias = jnp.broadcast_to(bias_ref[...], (ROWS, ROWS))
-
-    def ids_of(step):
-        return ids[pl.ds(ring(step), 1), :]
-
-    own_ids = jnp.broadcast_to(ids_of(0), (ROWS, ROWS)).T
-
-    def window_terms(left_emb, blocks, with_totals):
-        weights = []
-        totals = [jnp.zeros((1, COLS), F32) for _ in range(3)]
+    def window_terms(left_emb, blocks):
+        weights, inners = [], []
         for number in range(WINDOW):
             inner = dot(left_emb, blocks[number], ((1,), (1,)))
             logits = scale * inner + bias
             matched = own_ids == ids_of(number - REACH)
+            gradient = softplus_parts(logits)[1] - matched.astype(F32)
+            weights.append((scale * gradient).astype(BF16))
+            inners.append(inner)
+        return jnp.concatenate(weights, axis=1), inners
+
+    def window_totals(inners):
+        totals = [jnp.zeros((1, COLS), F32) for _ in range(3)]
+        for number, inner in enumerate(inners):
+            logits = scale * inner + bias
+            matched = own_ids == ids_of(number - REACH)
             tail, sigmoid = softplus_parts(logits)
             gradient = sigmoid - matched.astype(F32)
-            weights.append((scale * gradient).astype(BF16))
-            if with_totals:
-                signed = jnp.where(matched, logits, -logits)
-                loss = tail - jnp.minimum(signed, 0.0)
-                for place, term in enumerate((loss, gradient, gradient * inner)):
-                    totals[place] = totals[place] + jnp.sum(term, axis=0, keepdims=True)
-        return jnp.concatenate(weights, axis=1), totals
-
-    weight, totals = window_terms(embs[REACH], poses, True)
+            loss = tail - jnp.minimum(jnp.where(matched, logits, -logits), 0.0)
+            for place, term in enumerate((loss, gradient, gradient * inner)):
+                totals[place] = totals[place] + jnp.sum(term, axis=0, keepdims=True)
+        return totals
+
+    weight, inners = window_terms(embs[REACH], poses)
     grad_img = dot(weight, poses[...].reshape(WINDOW * ROWS, WIDTH), ((1,), (0,)))
     unit_img = unit[...]
     along = jnp.sum(unit_img * grad_img, axis=1, keepdims=True)
@@ -351,7 +358,7 @@
         gp_copies.append(copy)
     gp[slot] = gp_src[slot]
 
-    tot_src[...] = jnp.zeros_like(tot_src)
+    totals = window_totals(inners)
     for place in range(3):
         tot_src[place : place + 1, :] = totals[place]
     tot_copies = []
@@ -405,7 +412,6 @@
     pltpu.make_async_copy(part.at[pl.ds(0, CELLS - 1)], part.at[pl.ds(0, CELLS - 1)], part_r).wait()
 
     summed = jnp.sum(part[...].astype(F32), axis=0)
-    fin_src[...] = jnp.zeros_like(fin_src)
     for number in range(GROUP):
         fin_src[number, 0:2, :] = summed[2 * number : 2 * number + 2, :]
     fin_copies = []
@@ -417,7 +423,7 @@
     fin[slot] = fin_src[slot]
 
     emb_finish()
-    pose_weight, _ = window_terms(poses[REACH], embs, False)
+    pose_weight, _ = window_terms(poses[REACH], embs)
     grad_pose = dot(pose_weight, embs[...].reshape(WINDOW * ROWS, WIDTH), ((1,), (0,)))
     inv_q = inv_pose[:, 0:1]
     unit_pose = pose_raw[...].astype(F32) * inv_q
@@ -436,13 +442,8 @@
     loss_ref[1] = jnp.sum(y_sum[1:2, :])
     scale_grad_ref[0] = jnp.sum(y_sum[2:3, :])
 
-    for copy in fin_copies:
-        copy.wait_recv()
-    for number in range(GROUP):
-        head_grad_ref[:, number * COLS : (number + 1) * COLS] = fin[number, 0:2, :]
-
     store_pose.wait()
-    for copy in piece_copies + proj_copies + gp_copies + fin_copies:
+    for copy in piece_copies + proj_copies + gp_copies:
         copy.wait_send()
     for copy in tot_copies + z_copies + y_copies:
         copy.wait_send()
@@ -452,6 +453,11 @@
     emb_drain()
     pltpu.make_async_copy(head.at[pl.ds(0, CELLS - 1)], head.at[pl.ds(0, CELLS - 1)], head_s).wait()
     pltpu.make_async_copy(part_src.at[pl.ds(0, CELLS - 1)], part_src.at[pl.ds(0, CELLS - 1)], part_s).wait()
+
+    for copy in fin_copies:
+        copy.wait()
+    for number in range(GROUP):
+        head_grad_ref[:, number * COLS : (number + 1) * COLS] = fin[number, 0:2, :]
 
 
 def local(features, head_rows, poses, match_ids, logit_scale, logit_bias):

time: 67.7 us -> 67.5 us (level)
  no operation moved by 1% of the time
where the time goes in v4:
time: 67.5 us; the launch traced here: 67.3 us
  Pallas kernels  61.7 us (91%)
  between operations  3.72 us (6%)
  local copies, waits for them, and re-layouts  1.84 us (3%)
    pallas_call x1, Pallas kernels, local(): pl.pallas_call(kernel, name='contrastive', out_shape=shapes, in_specs=[hb...  61.7 us
    unnamed x5, local copies, waits for them, and re-layouts  1.84 us

profile of v4, /device:TPU:1, one launch (start us, length us, event | category | flops | bytes accessed | tf_op | source)
XLA Modules:
  0.0 67.3 jit_solution(17396810413676720973)
XLA Ops:
  1.3 0.0 copy-start
  1.9 0.0 copy-done
  2.0 61.7 %contrastive.1 = (bf16[128,1024]{1,0:T(8,128)(2,1)S(1)}, f32[2,1024]{1,0:T(2,128)S(1)}, f32[2]{0:T(128)S(1)}, f32[1]{0:T(128)}) custom-call(bf16[128,1024]{1,0:T(8,128)(2,1)} %feat_hbm.1, bf16[2,1024]{1,0:T(2,128)(2,1)S(1)} %copy-done, bf16[128,1024]{1,0:T(8,128)(2,1)} %pose_hbm.1, s32[512,128]{1,0:T(8,128)} %bitcast.5, f32[1,1]{1,0:T(1,128)} %bitcast.3.scale_ref, ...), custom_call_target="tpu_custom_call" | custom-call | tf_op jit(solution)/shard_map/contrastive/pallas_call | solution.py:476
  63.7 0.7 %copy.16 = bf16[128,1024]{1,0:T(8,128)(2,1)} copy(bf16[128,1024]{1,0:T(8,128)(2,1)S(1)} %get-tuple-element.8) | data formatting | bytes 524288
  64.4 0.6 copy.17
  65.0 0.5 copy.18
Async XLA Ops:
  1.3 0.7 %copy-start = (bf16[2,1024]{1,0:T(2,128)(2,1)S(1)}, bf16[2,1024]{1,0:T(2,128)(2,1)}, u32[]{:S(2)}) copy-start(bf16[2,1024]{1,0:T(2,128)(2,1)} %head_hbm.1) | copy-start | bytes 12292

commit v5 on v4

--- a/solution.py
+++ b/solution.py
@@ -52,8 +52,8 @@
 
 def kernel(
     feat_hbm, head_hbm, pose_hbm, ids_hbm, scale_ref, bias_ref,
-    pose_grad_hbm, head_grad_ref, loss_ref, scale_grad_ref,
-    feats, feats_t, pose_raw, poses, embs, pose_held, emb_held, pose_out, ids, head_rows, piece_src, piece, tile_f32, head,
+    pose_grad_ref, head_grad_ref, loss_ref, scale_grad_ref,
+    feats, feats_t, pose_raw, poses, embs, pose_held, emb_held, ids, head_rows, piece_src, piece, tile_f32, head,
     proj_src, proj, peak_src, peaks, peak_rows, unit, inv_pose, gp_src, gp, part_src, part, fin_src, fin,
     tot_src, tot_group, tot_z_src, tot_z, tot_y_src, tot_y,
     local_sem, piece_s, piece_r, feat_s, feat_r, head_s, head_r, pose_s, pose_r, emb_s, emb_r,
@@ -428,9 +428,7 @@
     inv_q = inv_pose[:, 0:1]
     unit_pose = pose_raw[...].astype(F32) * inv_q
     along_pose = jnp.sum(unit_pose * grad_pose, axis=1, keepdims=True)
-    pose_out[...] = ((grad_pose - unit_pose * along_pose) * inv_q).astype(BF16)
-    store_pose = pltpu.make_async_copy(pose_out, pose_grad_hbm, local_sem.at[4])
-    store_pose.start()
+    pose_grad_ref[...] = ((grad_pose - unit_pose * along_pose) * inv_q).astype(BF16)
 
     for copy in y_copies:
         copy.wait_recv()
@@ -442,7 +440,6 @@
     loss_ref[1] = jnp.sum(y_sum[1:2, :])
     scale_grad_ref[0] = jnp.sum(y_sum[2:3, :])
 
-    store_pose.wait()
     for copy in piece_copies + proj_copies + gp_copies:
         copy.wait_send()
     for copy in tot_copies + z_copies + y_copies:
@@ -478,14 +475,13 @@
         name="contrastive",
         out_shape=shapes,
         in_specs=[hbm, hbm, hbm, hbm, vmem, vmem],
-        out_specs=(hbm, vmem, smem, smem),
+        out_specs=(vmem, vmem, smem, smem),
         scratch_shapes=[
             pltpu.VMEM((GROUP,) + block, BF16),
             pltpu.VMEM((WIDTH, GROUP * ROWS), BF16),
             pltpu.VMEM(block, BF16),
             pltpu.VMEM((WINDOW,) + block, BF16),
             pltpu.VMEM((WINDOW,) + block, BF16),
-            pltpu.VMEM(block, BF16),
             pltpu.VMEM(block, BF16),
             pltpu.VMEM(block, BF16),
             pltpu.VMEM((COUNT, ROWS), jnp.int32),
@@ -513,7 +509,7 @@
             pltpu.VMEM((SIDE, 8, COLS), F32),
             pltpu.VMEM((8, COLS), F32),
             pltpu.VMEM((SIDE, 8, COLS), F32),
-            dma((5,)),
+            dma((4,)),
             dma((GROUP,)), dma((GROUP,)),
             dma((10,)), dma((10,)),
             dma, dma,

time: 67.5 us -> 67.4 us (level)
  no operation moved by 1% of the time
where the time goes in v5:
time: 67.4 us; the launch traced here: 67.3 us
  Pallas kernels  61.7 us (92%)
  between operations  3.72 us (6%)
  local copies, waits for them, and re-layouts  1.84 us (3%)
    pallas_call x1, Pallas kernels, local(): pl.pallas_call(kernel, name='contrastive', out_shape=shapes, in_specs=[hb...  61.7 us
    unnamed x5, local copies, waits for them, and re-layouts  1.84 us

profile of v5, /device:TPU:1, one launch (start us, length us, event | category | flops | bytes accessed | tf_op | source)
XLA Modules:
  0.0 67.3 jit_solution(16716173431679334991)
XLA Ops:
  1.3 0.0 copy-start
  1.9 0.0 copy-done
  2.0 61.7 %contrastive.1 = (bf16[128,1024]{1,0:T(8,128)(2,1)S(1)}, f32[2,1024]{1,0:T(2,128)S(1)}, f32[2]{0:T(128)S(1)}, f32[1]{0:T(128)}) custom-call(bf16[128,1024]{1,0:T(8,128)(2,1)} %feat_hbm.1, bf16[2,1024]{1,0:T(2,128)(2,1)S(1)} %copy-done, bf16[128,1024]{1,0:T(8,128)(2,1)} %pose_hbm.1, s32[512,128]{1,0:T(8,128)} %bitcast.5, f32[1,1]{1,0:T(1,128)} %bitcast.3.scale_ref, ...), custom_call_target="tpu_custom_call" | custom-call | tf_op jit(solution)/shard_map/contrastive/pallas_call | solution.py:473
  63.7 0.7 %copy.16 = bf16[128,1024]{1,0:T(8,128)(2,1)} copy(bf16[128,1024]{1,0:T(8,128)(2,1)S(1)} %get-tuple-element.8) | data formatting | bytes 524288
  64.4 0.6 copy.17
  65.0 0.5 copy.18
Async XLA Ops:
  1.3 0.7 %copy-start = (bf16[2,1024]{1,0:T(2,128)(2,1)S(1)}, bf16[2,1024]{1,0:T(2,128)(2,1)}, u32[]{:S(2)}) copy-start(bf16[2,1024]{1,0:T(2,128)(2,1)} %head_hbm.1) | copy-start | bytes 12292
